TPU v7x, 512 devices: a whole 4x4x16 slice. The times are simulated.
512 devices in a mesh: grp: 16 (over x, y), batch: 8 (over z_lo), tp: 4 (over z_hi, core).
Axes of the slice: x: 4, y: 4, z: 16 (z_hi: 2, z_lo: 8; z = z_hi * 8 + z_lo), core: 2. Of those that a mesh axis runs over, the one named last changes fastest.
Arguments:
- prefix_q: bfloat16 [8192, 8192], P(('batch', 'grp'), 'tp'), parts along dimension 0, may hold values from -6 to 6
- prefix_k: bfloat16 [8192, 1024], P(('batch', 'grp'), 'tp'), parts along dimension 0, may hold values from -6 to 6
- prefix_v: bfloat16 [8192, 1024], P(('batch', 'grp'), 'tp'), parts along dimension 0, may hold values from -6 to 6
- resp_q: bfloat16 [128, 128, 8192], P(('batch', 'grp'), None, 'tp'), parts along dimension 0, may hold values from -6 to 6
- resp_k: bfloat16 [128, 128, 1024], P(('batch', 'grp'), None, 'tp'), parts along dimension 0, may hold values from -6 to 6
- resp_v: bfloat16 [128, 128, 1024], P(('batch', 'grp'), None, 'tp'), parts along dimension 0, may hold values from -6 to 6
- lengths: int32 [128], P(('batch', 'grp')), parts along dimension 0, may hold values from 64 to 128, as said below
- d_prefix_out: bfloat16 [8192, 8192], P(('batch', 'grp'), 'tp'), parts along dimension 0, may hold values from -6 to 6
- d_resp_out: bfloat16 [128, 128, 8192], P(('batch', 'grp'), None, 'tp'), parts along dimension 0, may hold values from -6 to 6
Outputs:
- grad_prefix_q: bfloat16 [8192, 8192], P(('batch', 'grp'), 'tp'), parts along dimension 0
- grad_prefix_k: bfloat16 [8192, 1024], P(('batch', 'grp'), 'tp'), parts along dimension 0
- grad_prefix_v: bfloat16 [8192, 1024], P(('batch', 'grp'), 'tp'), parts along dimension 0
- grad_resp_q: bfloat16 [128, 128, 8192], P(('batch', 'grp'), None, 'tp'), parts along dimension 0
- grad_resp_k: bfloat16 [128, 128, 1024], P(('batch', 'grp'), None, 'tp'), parts along dimension 0
- grad_resp_v: bfloat16 [128, 128, 1024], P(('batch', 'grp'), None, 'tp'), parts along dimension 0
There are 8 independent parts, one for each index of `batch`. A program takes and returns all parts, laid end to end along the dimension named above; each array names one. Nothing has to cross between parts.
Inputs may be any that keep to these rules, and one draw needn't show every extreme that they name: `lengths`: each response's length; some response has exactly 128 tokens in every draw.
All inputs are finite; a program needn't handle non-finite values.
Results may differ from a plain program's by a relative error of at most 0.019.
Values may be sent and summed in bfloat16 or wider, within the bound.
No kernel may reach another device: no remote copies, remote signals or barrier semaphores. Data moves between devices by JAX's collectives and lax.ppermute only.
A program may use at most 64 MiB of HBM per device.

v0:
```python
import math

import jax
import jax.numpy as jnp
from jax import lax
from jax.sharding import PartitionSpec as P

HQ = 64
KVH = 8
HD = 128


masked_value = -1e30


def scores(query_head, key_head, visible):
    logits = jnp.einsum("qd,kd->qk", query_head, key_head, preferred_element_type=jnp.float32)
    logits = logits * (1.0 / math.sqrt(HD))
    return jnp.where(visible, logits, masked_value)


def logit_terms(weights, row_dot, grad_head, value_head):
    grad_logit = jnp.einsum("qd,kd->qk", grad_head, value_head, preferred_element_type=jnp.float32)
    logit_grad = weights * (grad_logit - row_dot[:, None])
    return logit_grad.astype(jnp.bfloat16)


def key_products(logit_low, weights_low, query_head, grad_head):
    key_grad = jnp.einsum("qk,qd->kd", logit_low, query_head, preferred_element_type=jnp.float32)
    key_grad = key_grad * (1.0 / math.sqrt(HD))
    value_grad = jnp.einsum("qk,qd->kd", weights_low, grad_head, preferred_element_type=jnp.float32)
    return (key_grad, value_grad)


def fold_heads(terms, kv_count, per_group):
    row_count = terms.shape[1]
    summed = terms.reshape(kv_count, per_group, row_count, HD).sum(1)
    return summed.transpose(1, 0, 2).reshape(row_count, kv_count * HD)


def on_device(
    prefix_q, prefix_k, prefix_v, resp_q, resp_k, resp_v, lengths, d_prefix_out, d_resp_out
):
    per_group = HQ // KVH
    head_count = prefix_q.shape[1] // HD
    kv_count = prefix_k.shape[1] // HD
    prefix_rows = prefix_q.shape[0]
    resp_rows = resp_q.shape[1]
    device_index = lax.axis_index("grp")
    gathered_keys, gathered_values = (
        lax.all_gather(prefix_k, "grp", axis=0, tiled=True),
        lax.all_gather(prefix_v, "grp", axis=0, tiled=True),
    )
    prefix_total = gathered_keys.shape[0]
    queries = jnp.concatenate([prefix_q, resp_q[0]], 0)
    keys_all = jnp.concatenate([gathered_keys, resp_k[0]], 0)
    values_all = jnp.concatenate([gathered_values, resp_v[0]], 0)
    positions = jnp.arange(resp_rows)
    live = positions < lengths[0]
    resp_grad = jnp.where(live[:, None], d_resp_out[0], jnp.zeros_like(d_resp_out[0]))
    out_grads = jnp.concatenate([d_prefix_out, resp_grad], 0)
    query_count = prefix_rows + resp_rows
    key_count = prefix_total + resp_rows
    query_pos = jnp.arange(query_count)[:, None]
    key_pos = jnp.arange(key_count)[None, :]
    in_prefix_key = key_pos < prefix_total
    prefix_visible = in_prefix_key & (key_pos <= device_index * prefix_rows + query_pos)
    resp_visible = in_prefix_key | (key_pos - prefix_total <= query_pos - prefix_rows)
    visible = jnp.where(query_pos < prefix_rows, prefix_visible, resp_visible)
    query_heads = queries.reshape(query_count, head_count, HD).transpose(1, 0, 2)
    grad_heads = out_grads.reshape(query_count, head_count, HD).transpose(1, 0, 2)
    key_heads = keys_all.reshape(key_count, kv_count, HD).transpose(1, 0, 2)
    value_heads = values_all.reshape(key_count, kv_count, HD).transpose(1, 0, 2)
    head_ids = jnp.arange(head_count)

    def per_head(item):
        query_head, grad_head, head_index = item
        key_head = lax.dynamic_index_in_dim(key_heads, head_index // per_group, 0, keepdims=False)
        value_head = lax.dynamic_index_in_dim(
            value_heads, head_index // per_group, 0, keepdims=False
        )
        logits = scores(query_head, key_head, visible)
        row_max = jnp.max(logits, 1)
        exponent = jnp.exp(logits - row_max[:, None])
        row_sum = jnp.sum(exponent, 1)
        weights = exponent / row_sum[:, None]
        weights_low = weights.astype(jnp.bfloat16)
        attended = jnp.dot(weights_low, value_head, preferred_element_type=jnp.float32)
        attended = lax.optimization_barrier(attended.astype(jnp.bfloat16))
        row_dot = jnp.sum(grad_head.astype(jnp.float32) * attended.astype(jnp.float32), 1)
        logit_low = logit_terms(weights, row_dot, grad_head, value_head)
        key_grad, value_grad = key_products(logit_low, weights_low, query_head, grad_head)
        query_grad = jnp.dot(logit_low, key_head, preferred_element_type=jnp.float32) * (
            1.0 / math.sqrt(HD)
        )
        return (query_grad.astype(jnp.bfloat16), key_grad, value_grad, row_max, row_sum, row_dot)

    query_grads, key_grads, value_grads, row_maxes, row_sums, row_dots = lax.map(
        per_head, (query_heads, grad_heads, head_ids)
    )
    query_flat = query_grads.transpose(1, 0, 2).reshape(query_count, head_count * HD)
    key_flat = fold_heads(key_grads, kv_count, per_group)
    value_flat = fold_heads(value_grads, kv_count, per_group)
    prefix_key_sum, prefix_value_sum = (
        lax.psum_scatter(
            key_flat[:prefix_total].astype(jnp.bfloat16), "grp", scatter_dimension=0, tiled=True
        ).astype(jnp.float32),
        lax.psum_scatter(
            value_flat[:prefix_total].astype(jnp.bfloat16), "grp", scatter_dimension=0, tiled=True
        ).astype(jnp.float32),
    )
    return (
        query_flat[:prefix_rows],
        prefix_key_sum.astype(jnp.bfloat16),
        prefix_value_sum.astype(jnp.bfloat16),
        query_flat[prefix_rows:][None],
        key_flat[prefix_total:].astype(jnp.bfloat16)[None],
        value_flat[prefix_total:].astype(jnp.bfloat16)[None],
    )


def solution(mesh):
    return jax.shard_map(
        on_device,
        mesh=mesh,
        in_specs=(
            P(("batch", "grp"), "tp"),
            P(("batch", "grp"), "tp"),
            P(("batch", "grp"), "tp"),
            P(("batch", "grp"), None, "tp"),
            P(("batch", "grp"), None, "tp"),
            P(("batch", "grp"), None, "tp"),
            P(("batch", "grp")),
            P(("batch", "grp"), "tp"),
            P(("batch", "grp"), None, "tp"),
        ),
        out_specs=(
            P(("batch", "grp"), "tp"),
            P(("batch", "grp"), "tp"),
            P(("batch", "grp"), "tp"),
            P(("batch", "grp"), None, "tp"),
            P(("batch", "grp"), None, "tp"),
            P(("batch", "grp"), None, "tp"),
        ),
        check_vma=False,
    )
```

profile of v0, /device:TPU:6, one launch (start us, length us, event | category | flops | bytes accessed | tf_op | source)
XLA Modules:
  0.0 442.9 jit_solution(81603987337864404)
XLA Ops:
  10.0 1.6 copy.66
  15.0 1.2 copy.81
  16.2 26.9 %all_gather.6 = bf16[1024,256]{1,0:T(8,128)(2,1)S(1)} all-gather(bf16[64,256]{1,0:T(8,128)(2,1)} %param.12), channel_id=1, replica_groups=mesh['grp'=16,'batch'=8,'tp'=4] {'grp'}, dimensions={0}, use_global_device_ids=true | all-gather | bytes 557056 | tf_op jit(solution)/shard_map/all_gather | solution.py:51
  43.4 21.8 %all_gather.7 = bf16[1024,256]{1,0:T(8,128)(2,1)S(1)} all-gather(bf16[64,256]{1,0:T(8,128)(2,1)} %param.13), channel_id=1, replica_groups=mesh['grp'=16,'batch'=8,'tp'=4] {'grp'}, dimensions={0}, use_global_device_ids=true | all-gather | bytes 557056 | tf_op jit(solution)/shard_map/all_gather | solution.py:52
  67.7 182.5 %while.17 = (s32[]{:T(128)}, bf16[16,192,128]{2,1,0:T(8,128)(2,1)}, f32[16,1152,128]{2,1,0:T(8,128)}, f32[16,1152,128]{2,1,0:T(8,128)}, bf16[16,192,128]{2,1,0:T...) while((s32[]{:T(128)}, bf16[16,192,128]{2,1,0:T(8,128)(2,1)}, ...), condition=%wide.region_4.5_spmd.clone, body=%wide.region_0.4_spmd.clone.sunk | while | flops 344702400 | bytes 8527713 | solution.py:98
  70.9 1.3 fusion.70
  75.8 2.1 fusion.75
  82.3 1.3 fusion.70
  87.2 2.1 fusion.75
  93.6 1.3 fusion.70
  98.5 2.1 fusion.75
  100.6 1.2 fusion.74
  105.0 1.3 fusion.70
  109.9 2.1 fusion.75
  112.0 1.2 fusion.74
  116.4 1.3 fusion.70
  121.3 2.1 fusion.75
  127.8 1.3 fusion.70
  132.7 2.1 fusion.75
  139.2 1.3 fusion.70
  144.1 2.2 fusion.75
  150.7 1.3 fusion.70
  155.6 2.1 fusion.75
  162.0 1.3 fusion.70
  166.9 2.1 fusion.75
  169.0 1.2 fusion.74
  173.4 1.3 fusion.70
  178.3 2.1 fusion.75
  180.4 1.2 fusion.74
  184.8 1.3 fusion.70
  189.7 2.1 fusion.75
  196.2 1.3 fusion.70
  201.1 2.1 fusion.75
  203.2 1.2 fusion.74
  207.6 1.3 fusion.70
  212.5 2.1 fusion.75
  219.0 1.3 fusion.70
  223.9 2.1 fusion.75
  230.4 1.3 fusion.70
  235.3 2.1 fusion.75
  237.4 1.3 fusion.74
  241.9 1.3 fusion.70
  246.8 2.1 fusion.75
  248.9 1.3 fusion.74
  250.2 4.2 bitcast_reduce_fusion
  255.7 4.2 bitcast_reduce_fusion.1
  265.1 78.6 %reduce-scatter.9.cloned.1.call-done = bf16[64,256]{1,0:T(8,128)(2,1)} async-done(((bf16[1024,256]{1,0:T(8,128)(2,1)}), bf16[64,256]{1,0:T(8,128)(2,1)}) %reduce-scatter.9.cloned.1.call-update) | async-done | bytes 32784
  343.8 92.2 %reduce-scatter.7.cloned.1.call-done = bf16[64,256]{1,0:T(8,128)(2,1)} async-done(((bf16[1024,256]{1,0:T(8,128)(2,1)}), bf16[64,256]{1,0:T(8,128)(2,1)}) %reduce-scatter.7.cloned.1.call-update) | async-done | bytes 32784
  (149 shorter events, 92.5 us)
Async XLA Ops:
  7.2 58.2 %copy-start.1 = (bf16[1,128,2048]{2,1,0:T(8,128)(2,1)S(1)}, bf16[1,128,2048]{2,1,0:T(8,128)(2,1)}, u32[]{:S(2)}) copy-start(bf16[1,128,2048]{2,1,0:T(8,128)(2,1)} %param.14) | copy-start | bytes 1572868
  7.2 336.6 %reduce-scatter.9.cloned.1.call-start = ((), (), s32[]{:S(2)}) async-start(), calls=%async_computation.3 | async-start | bytes 557056
  254.4 7.7 %copy-start = (bf16[16,192,128]{2,1,0:T(8,128)(2,1)S(1)}, bf16[16,192,128]{2,1,0:T(8,128)(2,1)}, u32[]{:S(2)}) copy-start(bf16[16,192,128]{2,1,0:T(8,128)(2,1)} %get-tuple-element.134) | copy-start | bytes 2359300
  255.7 180.3 %reduce-scatter.7.cloned.1.call-start = ((), (), s32[]{:S(2)}) async-start(), calls=%async_computation.2 | async-start | bytes 557056
Sparse Core Ops, SparseCore 0:
  255.8 87.9 reduce-scatter.8
  348.9 87.0 reduce-scatter.6
where the time goes:
time: 447 us; the launch traced here: 443 us
  waiting for transfers between devices  171 us (38%)
  matrix products  112 us (25%)
  blocking collectives  48.7 us (11%)
  loops' own time  42.1 us (9%)
  other arithmetic  32.3 us (7%)
  local copies, waits for them, and re-layouts  22 us (5%)
  between operations  14.9 us (3%)
    unnamed x4, waiting for transfers between devices  171 us
    another operation x1, loops' own time, on_device(): lax.map(per_head, (query_heads, grad_heads, head_ids))  42.1 us
    dot_general x16, matrix products, key_products(): jnp.einsum('qk,qd->kd', weights_low, grad_head, preferred_element_type=jn...  33.7 us
    all_gather x1, blocking collectives, on_device(): lax.all_gather(prefix_k, 'grp', axis=0, tiled=True)  26.9 us
    all_gather x1, blocking collectives, on_device(): lax.all_gather(prefix_v, 'grp', axis=0, tiled=True)  21.8 us
    dot_general x16, matrix products, scores(): jnp.einsum('qd,kd->qk', query_head, key_head, preferred_element_type=jnp....  20.2 us
    dot_general x16, matrix products, key_products(): jnp.einsum('qk,qd->kd', logit_low, query_head, preferred_element_type=jnp...  19.4 us
    dot_general x16, matrix products, logit_terms(): jnp.einsum('qd,kd->qk', grad_head, value_head, preferred_element_type=jnp...  18.1 us
  transfers between devices with their start and end apart: 2, of which 2 were waited for; matrix products, arithmetic and copies ran while one was open for 2% of the time, Pallas kernels for 0%

commit v1 on v0

v1 whole, which is shorter than its diff:
```python
import math

import jax
import jax.numpy as jnp
from jax import lax
from jax.experimental import pallas as pl
from jax.experimental.pallas import tpu as pltpu
from jax.sharding import PartitionSpec as P

HQ = 64
KVH = 8
HD = 128
per_group = HQ // KVH
scale = 1.0 / math.sqrt(HD)
scale_log2 = scale * math.log2(math.e)
masked_value = -1e30
unit = 256
step = 64
low = jnp.bfloat16


def dot(a, b):
    return jnp.dot(a, b, preferred_element_type=jnp.float32)


def dot_rows(a, b):
    return lax.dot_general(a, b, (((1,), (1,)), ((), ())), preferred_element_type=jnp.float32)


def together(copies):
    for copy in copies:
        copy.start()
    for copy in copies:
        copy.wait()


def spread_body(k, v, out, block, sems):
    rows, columns = k.shape
    block[:, 0:columns] = k[...]
    block[:, columns : 2 * columns] = v[...]
    together(
        [
            pltpu.make_async_copy(block, out.at[d * rows : (d + 1) * rows, :], sems.at[d])
            for d in range(out.shape[0] // rows)
        ]
    )


def stack_body(info, pq, rq, pdo, rdo, rk, rv, qs, dos, own, query_pos, qs_out, dos_out, sems):
    resp_rows = rq.shape[0]
    prefix_rows = pq.shape[0]
    span = per_group * (resp_rows + prefix_rows)
    columns = rk.shape[1]
    moves = [(rk, own.at[:, 0:columns]), (rv, own.at[:, columns : 2 * columns])]
    for h in range(pq.shape[1] // HD):
        part = slice(h * HD, (h + 1) * HD)
        first = h // per_group * span + h % per_group * resp_rows
        at = slice(first, first + resp_rows)
        moves += [(rq.at[:, part], qs.at[at, :]), (rdo.at[:, part], dos.at[at, :])]
        first = h // per_group * span + per_group * resp_rows + h % per_group * prefix_rows
        at = slice(first, first + prefix_rows)
        moves += [(pq.at[:, part], qs.at[at, :]), (pdo.at[:, part], dos.at[at, :])]
    together([pltpu.make_async_copy(a, b, sems.at[i]) for i, (a, b) in enumerate(moves)])
    live = lax.broadcasted_iota(jnp.int32, (resp_rows, HD), 0) < info[1]
    for h in range(pq.shape[1] // HD):
        first = h // per_group * span + h % per_group * resp_rows
        at = slice(first, first + resp_rows)
        dos[at, :] = jnp.where(live, dos[at, :], jnp.zeros((), low))
    together([pltpu.make_async_copy(a, b, sems.at[i]) for i, (a, b) in enumerate(((qs, qs_out), (dos, dos_out)))])
    query_pos[...] = info[0] + lax.broadcasted_iota(jnp.int32, query_pos.shape, 1) % prefix_rows


def hide_later(logits, at, prefix_total, is_resp, resp_rows, query_pos):
    if is_resp and at < prefix_total:
        return logits
    key_pos = lax.broadcasted_iota(jnp.int32, logits.shape, 0)
    if is_resp:
        last = lax.broadcasted_iota(jnp.int32, logits.shape, 1) % resp_rows - (at - prefix_total)
    else:
        last = query_pos[0:1, :] - at
    return jnp.where(key_pos <= last, logits, masked_value)


def attend_body(resp_all, kv, own, qs, dos, query_pos, terms, stats, ps, ds, dkv, s_ref, g_ref, qi, doi, ks, vs, sems):
    prefix_total = kv.shape[0]
    resp_rows = own.shape[0]
    columns = own.shape[1] // 2
    key_count = prefix_total + resp_rows
    heads = columns // HD
    row_count = qs.shape[0] // heads
    copies = []

    def send(columns):
        copy = pltpu.make_async_copy(dkv.at[:, columns], terms.at[:, columns], sems.at[len(copies)])
        copy.start()
        copies.append(copy)

    def fold(x):
        return jnp.sum(x.reshape(x.shape[0] // 8, 8, unit), 0)

    for h in range(heads):
        k_at = slice(h * HD, (h + 1) * HD)
        v_at = slice(columns + h * HD, columns + (h + 1) * HD)
        ks[h, 0:prefix_total, :] = kv[:, k_at]
        ks[h, prefix_total:, :] = own[:, k_at]
        vs[h, 0:prefix_total, :] = kv[:, v_at]
        vs[h, prefix_total:, :] = own[:, v_at]
        for start in range(0, row_count, unit):
            rows = slice(start, start + unit)
            slot = start // unit % 2
            is_resp = start < resp_all
            count = key_count if is_resp else prefix_total
            query = qs[h * row_count + start : h * row_count + start + unit, :]
            out_grad = dos[h * row_count + start : h * row_count + start + unit, :]
            logits = dot_rows(ks[h, 0:count, :], query)
            top = None
            for at in range(0, count, step):
                part = logits[at : at + step]
                part = hide_later(part, at, prefix_total, is_resp, resp_rows, query_pos)
                s_ref[slot, at : at + step, :] = part
                here = jnp.max(part.reshape(step // 8, 8, unit), 0)
                top = here if top is None else jnp.maximum(top, here)
            g_ref[slot, 0:count, :] = dot_rows(vs[h, 0:count, :], out_grad)
            shift = jnp.max(top, 0, keepdims=True) * scale_log2
            row_sum = jnp.zeros((8, unit), jnp.float32)
            row_dot = jnp.zeros((8, unit), jnp.float32)
            for at in range(0, count, step):
                exponent = jnp.exp2(s_ref[slot, at : at + step, :] * scale_log2 - shift)
                row_sum += fold(exponent)
                row_dot += fold(exponent * g_ref[slot, at : at + step, :])
                if at < prefix_total:
                    ps[h, at : at + step, rows] = exponent.astype(low)
            inverse = 1.0 / jnp.sum(row_sum, 0, keepdims=True)
            row_dot = jnp.sum(row_dot, 0, keepdims=True) * inverse
            stats[8 * h : 8 * h + 1, rows] = shift
            stats[8 * h + 1 : 8 * h + 2, rows] = inverse
            stats[8 * h + 2 : 8 * h + 3, rows] = row_dot
            by_row = jnp.broadcast_to(inverse, (HD, unit)).T
            qi[h, rows, :] = (query.astype(jnp.float32) * by_row).astype(low)
            doi[h, rows, :] = (out_grad.astype(jnp.float32) * by_row).astype(low)
            for at in range(0, prefix_total, step):
                exponent = ps[h, at : at + step, rows].astype(jnp.float32)
                ds[h, at : at + step, rows] = (exponent * (g_ref[slot, at : at + step, :] - row_dot)).astype(low)
        dkv[:, v_at] = dot(ps[h], doi[h]).astype(low)
        send(v_at)
        dkv[:, k_at] = (dot(ds[h], qi[h]) * scale).astype(low)
        send(k_at)
    for copy in copies:
        copy.wait()


def finish_body(resp_all, kv, own, query_pos, stats, qs_in, dos_in, dpq, drq, drk, drv, qs, dos, ks, vs, kt, pw, dw, sems):
    together([pltpu.make_async_copy(a, b, sems.at[i]) for i, (a, b) in enumerate(((qs_in, qs), (dos_in, dos)))])
    prefix_total = kv.shape[0]
    resp_rows = own.shape[0]
    columns = own.shape[1] // 2
    heads = columns // HD
    row_count = qs.shape[0] // heads
    prefix_rows = dpq.shape[0]
    for h in range(heads):
        k_at = slice(h * HD, (h + 1) * HD)
        v_at = slice(columns + h * HD, columns + (h + 1) * HD)
        ks[0:prefix_total, :] = kv[:, k_at]
        ks[prefix_total:, :] = own[:, k_at]
        vs[0:prefix_total, :] = kv[:, v_at]
        vs[prefix_total:, :] = own[:, v_at]
        kt[...] = ks[...].T
        for start in range(0, row_count, unit):
            rows = slice(start, start + unit)
            is_resp = start < resp_all
            count = prefix_total + resp_rows if is_resp else prefix_total
            shift = stats[8 * h : 8 * h + 1, rows]
            inverse = stats[8 * h + 1 : 8 * h + 2, rows]
            row_dot = stats[8 * h + 2 : 8 * h + 3, rows]
            logits = dot_rows(ks[0:count, :], qs[h * row_count + start : h * row_count + start + unit, :])
            grad_logit = dot_rows(vs[0:count, :], dos[h * row_count + start : h * row_count + start + unit, :])
            slopes = []
            for at in range(0, count, step):
                part = hide_later(logits[at : at + step], at, prefix_total, is_resp, resp_rows, query_pos)
                weights = jnp.exp2(part * scale_log2 - shift) * inverse
                slope = (weights * (grad_logit[at : at + step] - row_dot)).astype(low)
                slopes.append(slope)
                if at >= prefix_total:
                    pw[at - prefix_total : at - prefix_total + step, rows] = weights.astype(low)
                    dw[at - prefix_total : at - prefix_total + step, rows] = slope
            grad = (dot(kt[:, 0:count], jnp.concatenate(slopes, 0)) * scale).astype(low).T
            if is_resp:
                out, size, first = drq, resp_rows, start
            else:
                out, size, first = dpq, prefix_rows, start - resp_all
            for j in range(unit // size):
                head = h * per_group + first // size + j
                out[:, head * HD : (head + 1) * HD] = grad[j * size : (j + 1) * size]
        span = slice(h * row_count, h * row_count + resp_all)
        drv[:, k_at] = dot(pw[...], dos[span, :]).astype(low)
        drk[:, k_at] = (dot(dw[...], qs[span, :]) * scale).astype(low)


def total_body(parts, k, v):
    rows, columns = k.shape
    total = parts[0:rows, :].astype(jnp.float32)
    for d in range(1, parts.shape[0] // rows):
        total += parts[d * rows : (d + 1) * rows, :].astype(jnp.float32)
    total = total.astype(low)
    k[...] = total[:, 0:columns]
    v[...] = total[:, columns : 2 * columns]


def array(*shape):
    return jax.ShapeDtypeStruct(shape, low)


anywhere = pl.BlockSpec(memory_space=pl.ANY)
near = pl.BlockSpec(memory_space=pltpu.VMEM)
scalars = pl.BlockSpec(memory_space=pltpu.SMEM)
params = pltpu.CompilerParams(vmem_limit_bytes=30 * 1024 * 1024)


def exchange(blocks):
    return lax.all_to_all(blocks, "grp", 0, 0, tiled=True)


def on_device(
    prefix_q, prefix_k, prefix_v, resp_q, resp_k, resp_v, lengths, d_prefix_out, d_resp_out
):
    devices = lax.axis_size("grp")
    prefix_rows, columns = prefix_k.shape
    resp_rows = resp_q.shape[1]
    heads = columns // HD
    prefix_total = devices * prefix_rows
    key_count = prefix_total + resp_rows
    resp_all = per_group * resp_rows
    row_count = resp_all + per_group * prefix_rows
    info = jnp.stack([lax.axis_index("grp").astype(jnp.int32) * prefix_rows, lengths[0]])
    spread = pl.pallas_call(
        spread_body,
        in_specs=[near] * 2,
        out_specs=anywhere,
        out_shape=pltpu.HBM((prefix_total, 2 * columns), low),
        scratch_shapes=[pltpu.VMEM((prefix_rows, 2 * columns), low), pltpu.SemaphoreType.DMA((devices,))],
        name="spread",
    )(prefix_k, prefix_v)
    kv = exchange(spread)
    qs, dos, own, query_pos, qs_far, dos_far = pl.pallas_call(
        stack_body,
        in_specs=[scalars] + [anywhere] * 6,
        out_specs=[near] * 4 + [anywhere] * 2,
        out_shape=[
            pltpu.VMEM((heads * row_count, HD), low),
            pltpu.VMEM((heads * row_count, HD), low),
            pltpu.VMEM((resp_rows, 2 * columns), low),
            pltpu.VMEM((8, unit), jnp.int32),
            pltpu.HBM((heads * row_count, HD), low),
            pltpu.HBM((heads * row_count, HD), low),
        ],
        scratch_shapes=[pltpu.SemaphoreType.DMA((2 + 4 * heads * per_group,))],
        name="stack",
    )(info, prefix_q, resp_q[0], d_prefix_out, d_resp_out[0], resp_k[0], resp_v[0])
    terms, stats = pl.pallas_call(
        lambda *refs: attend_body(resp_all, *refs),
        in_specs=[near] * 5,
        out_specs=[anywhere, near],
        out_shape=[
            pltpu.HBM((prefix_total, 2 * columns), low),
            jax.ShapeDtypeStruct((8 * heads, row_count), jnp.float32),
        ],
        scratch_shapes=[
            pltpu.VMEM((heads, prefix_total, row_count), low),
            pltpu.VMEM((heads, prefix_total, row_count), low),
            pltpu.VMEM((prefix_total, 2 * columns), low),
            pltpu.VMEM((2, key_count, unit), jnp.float32),
            pltpu.VMEM((2, key_count, unit), jnp.float32),
            pltpu.VMEM((heads, row_count, HD), low),
            pltpu.VMEM((heads, row_count, HD), low),
            pltpu.VMEM((heads, key_count, HD), low),
            pltpu.VMEM((heads, key_count, HD), low),
            pltpu.SemaphoreType.DMA((2 * heads,)),
        ],
        compiler_params=params,
        name="attend",
    )(kv, own, qs, dos, query_pos)
    parts = exchange(terms)
    grad_prefix_q, grad_resp_q, grad_resp_k, grad_resp_v = pl.pallas_call(
        lambda *refs: finish_body(resp_all, *refs),
        in_specs=[near] * 4 + [anywhere] * 2,
        out_specs=[near] * 4,
        out_shape=[array(*prefix_q.shape), array(*resp_q.shape[1:])] + [array(resp_rows, columns)] * 2,
        scratch_shapes=[
            pltpu.VMEM((heads * row_count, HD), low),
            pltpu.VMEM((heads * row_count, HD), low),
            pltpu.VMEM((key_count, HD), low),
            pltpu.VMEM((key_count, HD), low),
            pltpu.VMEM((HD, key_count), low),
            pltpu.VMEM((resp_rows, resp_all), low),
            pltpu.VMEM((resp_rows, resp_all), low),
            pltpu.SemaphoreType.DMA((2,)),
        ],
        compiler_params=params,
        name="finish",
    )(kv, own, query_pos, stats, qs_far, dos_far)
    grad_prefix_k, grad_prefix_v = pl.pallas_call(
        total_body, in_specs=[near], out_specs=[near] * 2, out_shape=[array(prefix_rows, columns)] * 2, name="total"
    )(pltpu.with_memory_space_constraint(parts, pltpu.VMEM))
    return (grad_prefix_q, grad_prefix_k, grad_prefix_v, grad_resp_q[None], grad_resp_k[None], grad_resp_v[None])


def solution(mesh):
    rows = P(("batch", "grp"), "tp")
    items = P(("batch", "grp"), None, "tp")
    return jax.shard_map(
        on_device,
        mesh=mesh,
        in_specs=(rows, rows, rows, items, items, items, P(("batch", "grp")), rows, items),
        out_specs=(rows, rows, rows, items, items, items),
        check_vma=False,
    )
```

time: 447 us -> 60.1 us (0.13)
  the two profiles are of different devices: /device:TPU:6 before, /device:TPU:448 now
where the time goes in v1:
time: 60.1 us; the launch traced here: 59.6 us
  Pallas kernels  25.5 us (42%)
  waiting for transfers between devices  19.4 us (32%)
  starting transfers between devices  11 us (18%)
  local copies, waits for them, and re-layouts  1.77 us (3%)
  between operations  1.37 us (2%)
    all_to_all x2, waiting for transfers between devices, exchange(): return lax.all_to_all(blocks, 'grp', 0, 0, tiled=True)  19.4 us
    pallas_call x1, Pallas kernels, on_device(): pl.pallas_call(lambda *refs: attend_body(resp_all, *refs), in_specs=[near...  11.9 us
    all_to_all x2, starting transfers between devices, exchange(): return lax.all_to_all(blocks, 'grp', 0, 0, tiled=True)  11 us
    pallas_call x1, Pallas kernels, on_device(): pl.pallas_call(lambda *refs: finish_body(resp_all, *refs), in_specs=[near...  7.15 us
    pallas_call x1, Pallas kernels, on_device(): pl.pallas_call(stack_body, in_specs=[scalars] + [anywhere] * 6, out_specs...  3.82 us
    pallas_call x1, Pallas kernels, on_device(): pl.pallas_call(spread_body, in_specs=[near] * 2, out_specs=anywhere, out_...  1.89 us
    unnamed x8, local copies, waits for them, and re-layouts  1.77 us
  transfers between devices with their start and end apart: 2, of which 2 were waited for; matrix products, arithmetic and copies ran while one was open for 1% of the time, Pallas kernels for 18%

profile of v1, /device:TPU:448, one launch (start us, length us, event | category | flops | bytes accessed | tf_op | source)
XLA Modules:
  0.0 59.6 jit_solution(4654020454239769710)
XLA Ops:
  0.6 1.9 %spread.1 = bf16[1024,512]{1,0:T(8,128)(2,1)} custom-call(bf16[64,256]{1,0:T(8,128)(2,1)} %k.1, bf16[64,256]{1,0:T(8,128)(2,1)} %v.1), custom_call_target="tpu_custom_call" | custom-call | tf_op jit(solution)/shard_map/spread/pallas_call | solution.py:235
  2.5 7.0 %all-to-all-start = ((bf16[16,64,512]{2,1,0:T(8,128)(2,1)}), bf16[16,64,512]{2,1,0:T(8,128)(2,1)S(1)}, u32[]{:S(2)}, u32[]{:S(2)}) async-start(bf16[16,64,512]{2,1,0:T(8,128)(2,1)} %bitcast.15), calls=%async_computation | async-start | bytes 2097152 | tf_op jit(solution)/shard_map/all_to_all | solution.py:220
  10.2 0.6 pad_add_fusion.info
  10.8 3.8 %stack.9 = (bf16[3072,128]{1,0:T(8,128)(2,1)S(1)}, bf16[3072,128]{1,0:T(8,128)(2,1)S(1)}, bf16[128,512]{1,0:T(8,128)(2,1)S(1)}, s32[8,256]{1,0:T(8,128)S(1)}, bf...) custom-call(s32[2]{0:T(128)} %pad_add_fusion.info, bf16[64,2048]{1,0:T(8,128)(2,1)} %pq.1, bf16[128,2048]{1,0:T(8,128)(2,1)} %bitcast.17, ...), custom_call_target="tpu_custom_call" | custom-call | tf_op jit(solution)/shard_map/stack/pallas_call | solution.py:244
  14.7 12.6 %all-to-all-done = bf16[16,64,512]{2,1,0:T(8,128)(2,1)S(1)} async-done(((bf16[16,64,512]{2,1,0:T(8,128)(2,1)}), bf16[16,64,512]{2,1,0:T(8,128)(2,1)S(1)}, u32[]{:S(2)}, u32[]{:S(2)}) %all-to-all-start) | async-done | bytes 1048608 | tf_op jit(solution)/shard_map/all_to_all | solution.py:220
  27.3 11.9 %attend.1 = (bf16[1024,512]{1,0:T(8,128)(2,1)}, f32[16,1536]{1,0:T(8,128)S(1)}) custom-call(bf16[1024,512]{1,0:T(8,128)(2,1)S(1)} %bitcast.12, bf16[128,512]{1,0:T(8,128)(2,1)S(1)} %get-tuple-element.20.refs_1_, bf16[3072,128]{1,0:T(8,128)(2,1)S(1)} %get-tuple-element.22.refs_2_, bf16[3072,128]{1,0:T(8,128)(2,1)S(1)} %get-tuple-element.23.refs_3_, ...), custom_call_target="tpu_custom_call" | custom-call | tf_op jit(solution)/shard_map/attend/pallas_call | solution.py:259
  39.2 0.0 copy-start.2
  39.2 0.6 %copy-done.2 = f32[16,1536]{1,0:T(8,128)} copy-done((f32[16,1536]{1,0:T(8,128)}, f32[16,1536]{1,0:T(8,128)S(1)}, u32[]{:S(2)}) %copy-start.2) | copy-done | bytes 98328
  39.8 0.0 copy-start
  39.8 0.0 copy-start.3
  39.8 4.0 %all-to-all-start.1 = ((bf16[16,64,512]{2,1,0:T(8,128)(2,1)}), bf16[16,64,512]{2,1,0:T(8,128)(2,1)S(1)}, u32[]{:S(2)}, u32[]{:S(2)}) async-start(bf16[16,64,512]{2,1,0:T(8,128)(2,1)} %bitcast.16), calls=%async_computation.1 | async-start | bytes 2097152 | tf_op jit(solution)/shard_map/all_to_all | solution.py:220
  43.8 0.0 copy-done
  43.8 0.0 copy-done.3
  43.8 0.0 copy-start.1
  43.8 1.1 %copy-done.1 = bf16[3072,128]{1,0:T(8,128)(2,1)S(1)} copy-done((bf16[3072,128]{1,0:T(8,128)(2,1)S(1)}, bf16[3072,128]{1,0:T(8,128)(2,1)}, u32[]{:S(2)}) %copy-start.1) | copy-done | bytes 786456
  45.0 7.1 %finish.1 = (bf16[64,2048]{1,0:T(8,128)(2,1)}, bf16[128,2048]{1,0:T(8,128)(2,1)}, bf16[128,256]{1,0:T(8,128)(2,1)}, bf16[128,256]{1,0:T(8,128)(2,1)}) custom-call(bf16[1024,512]{1,0:T(8,128)(2,1)S(1)} %bitcast.13, bf16[128,512]{1,0:T(8,128)(2,1)S(1)} %get-tuple-element.20.refs_1_, s32[8,256]{1,0:T(8,128)S(1)} %get-tuple-element.21.refs_4_.refs_2_, ...), custom_call_target="tpu_custom_call" | custom-call | tf_op jit(solution)/shard_map/finish/pallas_call | solution.py:283
  52.1 6.8 %all-to-all-done.1 = bf16[16,64,512]{2,1,0:T(8,128)(2,1)S(1)} async-done(((bf16[16,64,512]{2,1,0:T(8,128)(2,1)}), bf16[16,64,512]{2,1,0:T(8,128)(2,1)S(1)}, u32[]{:S(2)}, u32[]{:S(2)}) %all-to-all-start.1) | async-done | bytes 1048608 | tf_op jit(solution)/shard_map/all_to_all | solution.py:220
  58.9 0.8 %total.1 = (bf16[64,256]{1,0:T(8,128)(2,1)}, bf16[64,256]{1,0:T(8,128)(2,1)}) custom-call(bf16[1024,512]{1,0:T(8,128)(2,1)S(1)} %bitcast.14), custom_call_target="tpu_custom_call" | custom-call | tf_op jit(solution)/shard_map/total/pallas_call | solution.py:301
Async XLA Ops:
  2.5 24.8 %all-to-all-start = ((bf16[16,64,512]{2,1,0:T(8,128)(2,1)}), bf16[16,64,512]{2,1,0:T(8,128)(2,1)S(1)}, u32[]{:S(2)}, u32[]{:S(2)}) async-start(bf16[16,64,512]{2,1,0:T(8,128)(2,1)} %bitcast.15), calls=%async_computation | async-start | bytes 2097152 | tf_op jit(solution)/shard_map/all_to_all | solution.py:220
  39.2 0.6 %copy-start.2 = (f32[16,1536]{1,0:T(8,128)}, f32[16,1536]{1,0:T(8,128)S(1)}, u32[]{:S(2)}) copy-start(f32[16,1536]{1,0:T(8,128)S(1)} %get-tuple-element.24.refs_3_) | copy-start | bytes 294916
  39.8 4.0 %copy-start = (bf16[3072,128]{1,0:T(8,128)(2,1)S(1)}, bf16[3072,128]{1,0:T(8,128)(2,1)}, u32[]{:S(2)}) copy-start(bf16[3072,128]{1,0:T(8,128)(2,1)} %get-tuple-element.25.refs_4_) | copy-start | bytes 2359300
  39.8 4.0 %copy-start.3 = (f32[16,1536]{1,0:T(8,128)S(1)}, f32[16,1536]{1,0:T(8,128)}, u32[]{:S(2)}) copy-start(f32[16,1536]{1,0:T(8,128)} %copy-done.2) | copy-start | bytes 294916
  39.8 19.0 %all-to-all-start.1 = ((bf16[16,64,512]{2,1,0:T(8,128)(2,1)}), bf16[16,64,512]{2,1,0:T(8,128)(2,1)S(1)}, u32[]{:S(2)}, u32[]{:S(2)}) async-start(bf16[16,64,512]{2,1,0:T(8,128)(2,1)} %bitcast.16), calls=%async_computation.1 | async-start | bytes 2097152 | tf_op jit(solution)/shard_map/all_to_all | solution.py:220
  43.8 1.1 %copy-start.1 = (bf16[3072,128]{1,0:T(8,128)(2,1)S(1)}, bf16[3072,128]{1,0:T(8,128)(2,1)}, u32[]{:S(2)}) copy-start(bf16[3072,128]{1,0:T(8,128)(2,1)} %get-tuple-element.26.refs_5_) | copy-start | bytes 2359300

commit v2 on v1

--- a/solution.py
+++ b/solution.py
@@ -16,6 +16,8 @@
 masked_value = -1e30
 unit = 256
 step = 64
+PIECES = 1
+GATHER = 1
 low = jnp.bfloat16
 
 
@@ -36,14 +38,14 @@
 
 def spread_body(k, v, out, block, sems):
     rows, columns = k.shape
-    block[:, 0:columns] = k[...]
-    block[:, columns : 2 * columns] = v[...]
+    devices = out.shape[0] // rows
     together(
         [
-            pltpu.make_async_copy(block, out.at[d * rows : (d + 1) * rows, :], sems.at[d])
-            for d in range(out.shape[0] // rows)
+            pltpu.make_async_copy(k, block.at[:, 0:columns], sems.at[devices]),
+            pltpu.make_async_copy(v, block.at[:, columns : 2 * columns], sems.at[devices + 1]),
         ]
     )
+    together([pltpu.make_async_copy(block, out.at[d * rows : (d + 1) * rows, :], sems.at[d]) for d in range(devices)])
 
 
 def stack_body(info, pq, rq, pdo, rdo, rk, rv, qs, dos, own, query_pos, qs_out, dos_out, sems):
@@ -81,13 +83,15 @@
     return jnp.where(key_pos <= last, logits, masked_value)
 
 
-def attend_body(resp_all, kv, own, qs, dos, query_pos, terms, stats, ps, ds, dkv, s_ref, g_ref, qi, doi, ks, vs, sems):
+def attend_body(resp_all, kv, own, qs, dos, query_pos, terms, stats_out, stats, ps, ds, dkv, s_ref, g_ref, qi, doi, ks, vs, sems):
     prefix_total = kv.shape[0]
     resp_rows = own.shape[0]
     columns = own.shape[1] // 2
     key_count = prefix_total + resp_rows
     heads = columns // HD
     row_count = qs.shape[0] // heads
+    units = [(h, start) for h in range(heads) for start in range(0, row_count, unit)]
+    tops = {}
     copies = []
 
     def send(columns):
@@ -98,55 +102,133 @@
     def fold(x):
         return jnp.sum(x.reshape(x.shape[0] // 8, 8, unit), 0)
 
-    for h in range(heads):
-        k_at = slice(h * HD, (h + 1) * HD)
-        v_at = slice(columns + h * HD, columns + (h + 1) * HD)
-        ks[h, 0:prefix_total, :] = kv[:, k_at]
-        ks[h, prefix_total:, :] = own[:, k_at]
-        vs[h, 0:prefix_total, :] = kv[:, v_at]
-        vs[h, prefix_total:, :] = own[:, v_at]
-        for start in range(0, row_count, unit):
-            rows = slice(start, start + unit)
-            slot = start // unit % 2
-            is_resp = start < resp_all
-            count = key_count if is_resp else prefix_total
-            query = qs[h * row_count + start : h * row_count + start + unit, :]
-            out_grad = dos[h * row_count + start : h * row_count + start + unit, :]
-            logits = dot_rows(ks[h, 0:count, :], query)
-            top = None
-            for at in range(0, count, step):
-                part = logits[at : at + step]
-                part = hide_later(part, at, prefix_total, is_resp, resp_rows, query_pos)
+    def k_at(h):
+        return slice(h * HD, (h + 1) * HD)
+
+    def v_at(h):
+        return slice(columns + h * HD, columns + (h + 1) * HD)
+
+    def count_of(u):
+        return key_count if units[u][1] < resp_all else prefix_total
+
+    def rows_of(u):
+        first = units[u][0] * row_count + units[u][1]
+        return slice(first, first + unit)
+
+    def products(u):
+        h, start = units[u]
+        slot = u % 2
+        count = count_of(u)
+        size = count // PIECES
+
+        def logits_of(first):
+            logits = dot_rows(ks[h, first : first + size, :], qs[rows_of(u), :])
+            for at in range(first, first + size, step):
+                part = logits[at - first : at - first + step]
+                part = hide_later(part, at, prefix_total, start < resp_all, resp_rows, query_pos)
                 s_ref[slot, at : at + step, :] = part
                 here = jnp.max(part.reshape(step // 8, 8, unit), 0)
-                top = here if top is None else jnp.maximum(top, here)
-            g_ref[slot, 0:count, :] = dot_rows(vs[h, 0:count, :], out_grad)
-            shift = jnp.max(top, 0, keepdims=True) * scale_log2
-            row_sum = jnp.zeros((8, unit), jnp.float32)
-            row_dot = jnp.zeros((8, unit), jnp.float32)
-            for at in range(0, count, step):
-                exponent = jnp.exp2(s_ref[slot, at : at + step, :] * scale_log2 - shift)
-                row_sum += fold(exponent)
-                row_dot += fold(exponent * g_ref[slot, at : at + step, :])
-                if at < prefix_total:
-                    ps[h, at : at + step, rows] = exponent.astype(low)
-            inverse = 1.0 / jnp.sum(row_sum, 0, keepdims=True)
-            row_dot = jnp.sum(row_dot, 0, keepdims=True) * inverse
+                tops[u] = jnp.maximum(tops[u], here) if u in tops else here
+
+        def grads_of(first):
+            g_ref[slot, first : first + size, :] = dot_rows(vs[h, first : first + size, :], dos[rows_of(u), :])
+
+        for first in range(0, count, size):
+            yield lambda first=first: logits_of(first)
+        for first in range(0, count, size):
+            yield lambda first=first: grads_of(first)
+
+    def weigh(u):
+        h, start = units[u]
+        slot = u % 2
+        rows = slice(start, start + unit)
+        shift = jnp.max(tops[u], 0, keepdims=True) * scale_log2
+        sums = [jnp.zeros((8, unit), jnp.float32), jnp.zeros((8, unit), jnp.float32)]
+
+        def exponents_of(at):
+            exponent = jnp.exp2(s_ref[slot, at : at + step, :] * scale_log2 - shift)
+            sums[0] += fold(exponent)
+            sums[1] += fold(exponent * g_ref[slot, at : at + step, :])
+            if at < prefix_total:
+                ps[h, at : at + step, rows] = exponent.astype(low)
+
+        def close():
+            inverse = 1.0 / jnp.sum(sums[0], 0, keepdims=True)
+            row_dot = jnp.sum(sums[1], 0, keepdims=True) * inverse
             stats[8 * h : 8 * h + 1, rows] = shift
             stats[8 * h + 1 : 8 * h + 2, rows] = inverse
             stats[8 * h + 2 : 8 * h + 3, rows] = row_dot
             by_row = jnp.broadcast_to(inverse, (HD, unit)).T
-            qi[h, rows, :] = (query.astype(jnp.float32) * by_row).astype(low)
-            doi[h, rows, :] = (out_grad.astype(jnp.float32) * by_row).astype(low)
-            for at in range(0, prefix_total, step):
-                exponent = ps[h, at : at + step, rows].astype(jnp.float32)
-                ds[h, at : at + step, rows] = (exponent * (g_ref[slot, at : at + step, :] - row_dot)).astype(low)
-        dkv[:, v_at] = dot(ps[h], doi[h]).astype(low)
-        send(v_at)
-        dkv[:, k_at] = (dot(ds[h], qi[h]) * scale).astype(low)
-        send(k_at)
+            qi[h, rows, :] = (qs[rows_of(u), :].astype(jnp.float32) * by_row).astype(low)
+            doi[h, rows, :] = (dos[rows_of(u), :].astype(jnp.float32) * by_row).astype(low)
+            sums.append(row_dot)
+
+        def slopes_of(at):
+            exponent = ps[h, at : at + step, rows].astype(jnp.float32)
+            ds[h, at : at + step, rows] = (exponent * (g_ref[slot, at : at + step, :] - sums[2])).astype(low)
+
+        for at in range(0, count_of(u), step):
+            yield lambda at=at: exponents_of(at)
+        yield close
+        for at in range(0, prefix_total, step):
+            yield lambda at=at: slopes_of(at)
+
+    def gather(h):
+        size = prefix_total // GATHER
+
+        def values_of(at):
+            dkv[at : at + size, v_at(h)] = dot(ps[h, at : at + size, :], doi[h]).astype(low)
+
+        def keys_of(at):
+            dkv[at : at + size, k_at(h)] = (dot(ds[h, at : at + size, :], qi[h]) * scale).astype(low)
+
+        for at in range(0, prefix_total, size):
+            yield lambda at=at: values_of(at)
+        yield lambda: send(v_at(h))
+        for at in range(0, prefix_total, size):
+            yield lambda at=at: keys_of(at)
+        yield lambda: send(k_at(h))
+
+    def weave(one, other):
+        one, other = list(one), list(other)
+        done = 0
+        for i, task in enumerate(one):
+            task()
+            until = (i + 1) * len(other) // len(one)
+            for j in range(done, until):
+                other[j]()
+            done = until
+
+    for h in range(heads):
+        ks[h, 0:prefix_total, :] = kv[:, k_at(h)]
+        ks[h, prefix_total:, :] = own[:, k_at(h)]
+        vs[h, 0:prefix_total, :] = kv[:, v_at(h)]
+        vs[h, prefix_total:, :] = own[:, v_at(h)]
+    for task in products(0):
+        task()
+    waiting = []
+    per_head = row_count // unit
+    for u in range(len(units)):
+        h = units[u][0]
+        beside = list(products(u + 1)) if u + 1 < len(units) else []
+        left = (h + 1) * per_head - u
+        take = -(-len(waiting) // left)
+        beside += waiting[:take]
+        waiting = waiting[take:]
+        if beside:
+            weave(weigh(u), beside)
+        else:
+            for task in weigh(u):
+                task()
+        if left == 1:
+            waiting += list(gather(h))
+    keep = pltpu.make_async_copy(stats, stats_out, sems.at[2 * heads])
+    keep.start()
+    for task in waiting:
+        task()
     for copy in copies:
         copy.wait()
+    keep.wait()
 
 
 def finish_body(resp_all, kv, own, query_pos, stats, qs_in, dos_in, dpq, drq, drk, drv, qs, dos, ks, vs, kt, pw, dw, sems):
@@ -234,10 +316,10 @@
     info = jnp.stack([lax.axis_index("grp").astype(jnp.int32) * prefix_rows, lengths[0]])
     spread = pl.pallas_call(
         spread_body,
-        in_specs=[near] * 2,
+        in_specs=[anywhere] * 2,
         out_specs=anywhere,
         out_shape=pltpu.HBM((prefix_total, 2 * columns), low),
-        scratch_shapes=[pltpu.VMEM((prefix_rows, 2 * columns), low), pltpu.SemaphoreType.DMA((devices,))],
+        scratch_shapes=[pltpu.VMEM((prefix_rows, 2 * columns), low), pltpu.SemaphoreType.DMA((devices + 2,))],
         name="spread",
     )(prefix_k, prefix_v)
     kv = exchange(spread)
@@ -259,12 +341,13 @@
     terms, stats = pl.pallas_call(
         lambda *refs: attend_body(resp_all, *refs),
         in_specs=[near] * 5,
-        out_specs=[anywhere, near],
+        out_specs=[anywhere] * 2,
         out_shape=[
             pltpu.HBM((prefix_total, 2 * columns), low),
-            jax.ShapeDtypeStruct((8 * heads, row_count), jnp.float32),
+            pltpu.HBM((8 * heads, row_count), jnp.float32),
         ],
         scratch_shapes=[
+            pltpu.VMEM((8 * heads, row_count), jnp.float32),
             pltpu.VMEM((heads, prefix_total, row_count), low),
             pltpu.VMEM((heads, prefix_total, row_count), low),
             pltpu.VMEM((prefix_total, 2 * columns), low),
@@ -274,7 +357,7 @@
             pltpu.VMEM((heads, row_count, HD), low),
             pltpu.VMEM((heads, key_count, HD), low),
             pltpu.VMEM((heads, key_count, HD), low),
-            pltpu.SemaphoreType.DMA((2 * heads,)),
+            pltpu.SemaphoreType.DMA((2 * heads + 1,)),
         ],
         compiler_params=params,
         name="attend",

time: 60.1 us -> 58.9 us (0.980)
  the two profiles are of different devices: /device:TPU:448 before, /device:TPU:416 now
where the time goes in v2:
time: 58.9 us; the launch traced here: 58.4 us
  Pallas kernels  24.9 us (42%)
  waiting for transfers between devices  19.4 us (33%)
  starting transfers between devices  11 us (19%)
  between operations  1.37 us (2%)
  local copies, waits for them, and re-layouts  1.14 us (2%)
  other arithmetic  0.59 us (1%)
    all_to_all x2, waiting for transfers between devices, exchange(): return lax.all_to_all(blocks, 'grp', 0, 0, tiled=True)  19.4 us
    pallas_call x1, Pallas kernels, on_device(): pl.pallas_call(lambda *refs: attend_body(resp_all, *refs), in_specs=[near...  11.3 us
    all_to_all x2, starting transfers between devices, exchange(): return lax.all_to_all(blocks, 'grp', 0, 0, tiled=True)  11 us
    pallas_call x1, Pallas kernels, on_device(): pl.pallas_call(lambda *refs: finish_body(resp_all, *refs), in_specs=[near...  7.14 us
    pallas_call x1, Pallas kernels, on_device(): pl.pallas_call(stack_body, in_specs=[scalars] + [anywhere] * 6, out_specs...  3.84 us
    pallas_call x1, Pallas kernels, on_device(): pl.pallas_call(spread_body, in_specs=[anywhere] * 2, out_specs=anywhere,...  1.91 us
  transfers between devices with their start and end apart: 2, of which 2 were waited for; matrix products, arithmetic and copies ran while one was open for 1% of the time, Pallas kernels for 19%

profile of v2, /device:TPU:416, one launch (start us, length us, event | category | flops | bytes accessed | tf_op | source)
XLA Modules:
  0.0 58.4 jit_solution(9024636428097799269)
XLA Ops:
  0.6 1.9 %spread.1 = bf16[1024,512]{1,0:T(8,128)(2,1)} custom-call(bf16[64,256]{1,0:T(8,128)(2,1)} %k.1, bf16[64,256]{1,0:T(8,128)(2,1)} %v.1), custom_call_target="tpu_custom_call" | custom-call | tf_op jit(solution)/shard_map/spread/pallas_call | solution.py:317
  2.5 7.0 %all-to-all-start = ((bf16[16,64,512]{2,1,0:T(8,128)(2,1)}), bf16[16,64,512]{2,1,0:T(8,128)(2,1)S(1)}, u32[]{:S(2)}, u32[]{:S(2)}) async-start(bf16[16,64,512]{2,1,0:T(8,128)(2,1)} %bitcast.15), calls=%async_computation | async-start | bytes 2097152 | tf_op jit(solution)/shard_map/all_to_all | solution.py:302
  10.3 0.6 %pad_add_fusion.info = s32[2]{0:T(128)} fusion(s32[1]{0:T(128)S(6)} %copy.15, s32[1]{0:T(128)} %bitcast.2), kind=kLoop, calls=%fused_computation | loop fusion | flops 2 | bytes 16 | tf_op jit(solution)/shard_map/stack | solution.py:316
  10.8 3.8 %stack.9 = (bf16[3072,128]{1,0:T(8,128)(2,1)S(1)}, bf16[3072,128]{1,0:T(8,128)(2,1)S(1)}, bf16[128,512]{1,0:T(8,128)(2,1)S(1)}, s32[8,256]{1,0:T(8,128)S(1)}, bf...) custom-call(s32[2]{0:T(128)} %pad_add_fusion.info, bf16[64,2048]{1,0:T(8,128)(2,1)} %pq.1, bf16[128,2048]{1,0:T(8,128)(2,1)} %bitcast.17, ...), custom_call_target="tpu_custom_call" | custom-call | tf_op jit(solution)/shard_map/stack/pallas_call | solution.py:326
  14.7 12.6 %all-to-all-done = bf16[16,64,512]{2,1,0:T(8,128)(2,1)S(1)} async-done(((bf16[16,64,512]{2,1,0:T(8,128)(2,1)}), bf16[16,64,512]{2,1,0:T(8,128)(2,1)S(1)}, u32[]{:S(2)}, u32[]{:S(2)}) %all-to-all-start) | async-done | bytes 1048608 | tf_op jit(solution)/shard_map/all_to_all | solution.py:302
  27.3 11.3 %attend.1 = (bf16[1024,512]{1,0:T(8,128)(2,1)}, f32[16,1536]{1,0:T(8,128)}) custom-call(bf16[1024,512]{1,0:T(8,128)(2,1)S(1)} %bitcast.12, bf16[128,512]{1,0:T(8,128)(2,1)S(1)} %get-tuple-element.20.refs_1_, bf16[3072,128]{1,0:T(8,128)(2,1)S(1)} %get-tuple-element.22.refs_2_, bf16[3072,128]{1,0:T(8,128)(2,1)S(1)} %get-tuple-element.23.refs_3_, ...), custom_call_target="tpu_custom_call" | custom-call | tf_op jit(solution)/shard_map/attend/pallas_call | solution.py:341
  38.6 0.0 copy-start
  38.6 0.0 copy-start.2
  38.6 4.0 %all-to-all-start.1 = ((bf16[16,64,512]{2,1,0:T(8,128)(2,1)}), bf16[16,64,512]{2,1,0:T(8,128)(2,1)S(1)}, u32[]{:S(2)}, u32[]{:S(2)}) async-start(bf16[16,64,512]{2,1,0:T(8,128)(2,1)} %bitcast.16), calls=%async_computation.1 | async-start | bytes 2097152 | tf_op jit(solution)/shard_map/all_to_all | solution.py:302
  42.6 0.0 copy-done
  42.6 0.0 copy-done.2
  42.6 0.0 copy-start.1
  42.6 1.1 %copy-done.1 = bf16[3072,128]{1,0:T(8,128)(2,1)S(1)} copy-done((bf16[3072,128]{1,0:T(8,128)(2,1)S(1)}, bf16[3072,128]{1,0:T(8,128)(2,1)}, u32[]{:S(2)}) %copy-start.1) | copy-done | bytes 786456
  43.7 7.1 %finish.1 = (bf16[64,2048]{1,0:T(8,128)(2,1)}, bf16[128,2048]{1,0:T(8,128)(2,1)}, bf16[128,256]{1,0:T(8,128)(2,1)}, bf16[128,256]{1,0:T(8,128)(2,1)}) custom-call(bf16[1024,512]{1,0:T(8,128)(2,1)S(1)} %bitcast.13, bf16[128,512]{1,0:T(8,128)(2,1)S(1)} %get-tuple-element.20.refs_1_, s32[8,256]{1,0:T(8,128)S(1)} %get-tuple-element.21.refs_4_.refs_2_, ...), custom_call_target="tpu_custom_call" | custom-call | tf_op jit(solution)/shard_map/finish/pallas_call | solution.py:366
  50.9 6.8 %all-to-all-done.1 = bf16[16,64,512]{2,1,0:T(8,128)(2,1)S(1)} async-done(((bf16[16,64,512]{2,1,0:T(8,128)(2,1)}), bf16[16,64,512]{2,1,0:T(8,128)(2,1)S(1)}, u32[]{:S(2)}, u32[]{:S(2)}) %all-to-all-start.1) | async-done | bytes 1048608 | tf_op jit(solution)/shard_map/all_to_all | solution.py:302
  57.6 0.8 %total.1 = (bf16[64,256]{1,0:T(8,128)(2,1)}, bf16[64,256]{1,0:T(8,128)(2,1)}) custom-call(bf16[1024,512]{1,0:T(8,128)(2,1)S(1)} %bitcast.14), custom_call_target="tpu_custom_call" | custom-call | tf_op jit(solution)/shard_map/total/pallas_call | solution.py:384
Async XLA Ops:
  2.5 24.8 %all-to-all-start = ((bf16[16,64,512]{2,1,0:T(8,128)(2,1)}), bf16[16,64,512]{2,1,0:T(8,128)(2,1)S(1)}, u32[]{:S(2)}, u32[]{:S(2)}) async-start(bf16[16,64,512]{2,1,0:T(8,128)(2,1)} %bitcast.15), calls=%async_computation | async-start | bytes 2097152 | tf_op jit(solution)/shard_map/all_to_all | solution.py:302
  38.6 4.0 %copy-start = (bf16[3072,128]{1,0:T(8,128)(2,1)S(1)}, bf16[3072,128]{1,0:T(8,128)(2,1)}, u32[]{:S(2)}) copy-start(bf16[3072,128]{1,0:T(8,128)(2,1)} %get-tuple-element.25.refs_4_) | copy-start | bytes 2359300
  38.6 4.0 %copy-start.2 = (f32[16,1536]{1,0:T(8,128)S(1)}, f32[16,1536]{1,0:T(8,128)}, u32[]{:S(2)}) copy-start(f32[16,1536]{1,0:T(8,128)} %get-tuple-element.24.refs_3_) | copy-start | bytes 294916
  38.6 19.0 %all-to-all-start.1 = ((bf16[16,64,512]{2,1,0:T(8,128)(2,1)}), bf16[16,64,512]{2,1,0:T(8,128)(2,1)S(1)}, u32[]{:S(2)}, u32[]{:S(2)}) async-start(bf16[16,64,512]{2,1,0:T(8,128)(2,1)} %bitcast.16), calls=%async_computation.1 | async-start | bytes 2097152 | tf_op jit(solution)/shard_map/all_to_all | solution.py:302
  42.6 1.1 %copy-start.1 = (bf16[3072,128]{1,0:T(8,128)(2,1)S(1)}, bf16[3072,128]{1,0:T(8,128)(2,1)}, u32[]{:S(2)}) copy-start(bf16[3072,128]{1,0:T(8,128)(2,1)} %get-tuple-element.26.refs_5_) | copy-start | bytes 2359300
